TPU v7x, 256 devices: a whole 4x4x8 slice. The times are simulated.
256 devices in a mesh: tm: 32 (over y_hi, z, core), space: 8 (over y_lo, x).
Axes of the slice: x: 4, y: 4 (y_hi: 2, y_lo: 2; y = y_hi * 2 + y_lo), z: 8, core: 2. Of those that a mesh axis runs over, the one named last changes fastest.
Arguments:
- query_tiles: bfloat16 [32, 8, 256, 1536], P('tm', 'space'), may hold values from -6 to 6
- key_tiles: bfloat16 [32, 8, 256, 1536], P('tm', 'space'), may hold values from -6 to 6
- value_tiles: bfloat16 [32, 8, 256, 1536], P('tm', 'space'), may hold values from -6 to 6
- grad_tiles: bfloat16 [32, 8, 256, 1536], P('tm', 'space'), may hold values from -6 to 6
- log_sums: float32 [32, 8, 12, 256], P('tm', 'space'), may hold values from 3 to 5
- row_delta: float32 [32, 8, 12, 256], P('tm', 'space'), may hold values from -24 to 24
- text_keys: bfloat16 [256, 1536], P('space'), may hold values from -6 to 6
- text_values: bfloat16 [256, 1536], P('space'), may hold values from -6 to 6
- touch_list: int32 [32, 8, 128], P('tm', 'space'), may hold values from 0 to 255, as said below
Outputs:
- query_grad: bfloat16 [32, 8, 256, 1536], P('tm', 'space')
- key_grad: bfloat16 [32, 8, 256, 1536], P('tm', 'space')
- value_grad: bfloat16 [32, 8, 256, 1536], P('tm', 'space')
- text_key_grad: bfloat16 [256, 1536], P('space')
- text_value_grad: bfloat16 [256, 1536], P('space')
Inputs may be any that keep to these rules, and one draw needn't show every extreme that they name: `touch_list`: every tile's list is the same: the prompt's 128 different non-padding text tokens.
All inputs are finite; a program needn't handle non-finite values.
Results may differ from a plain program's by a relative error of at most 0.006.
Values may be sent and summed in bfloat16 or wider, within the bound.
A program may use at most 128 MiB of HBM per device.

v0:
```python
import jax
import jax.numpy as jnp
from jax import lax
from jax.sharding import PartitionSpec as P


def extended(block, sides, width):
    for axis, dim in sides:
        count = lax.axis_size(axis)
        forward = [(i, i + 1) for i in range(count - 1)]
        backward = [(target, source) for source, target in forward]
        low = lax.ppermute(
            lax.slice_in_dim(block, block.shape[dim] - width, None, axis=dim), axis, forward
        )
        high = lax.ppermute(lax.slice_in_dim(block, 0, width, axis=dim), axis, backward)
        block = jnp.concatenate([low, block, high], axis=dim)
    return block


def from_behind(value, axis, steps):
    count = lax.axis_size(axis)
    leading, last = (max(0, -steps), min(count, count - steps))
    return lax.ppermute(value, axis, [(source, source + steps) for source in range(leading, last)])


def rounded(values_in):
    return lax.optimization_barrier(values_in.astype(jnp.bfloat16)).astype(jnp.float32)


def block_grads(queries, key_rows, value_rows, grad_rows, saved_sums, saved_delta, retain):
    row_count, feature_width = queries.shape
    head_count = saved_sums.shape[0]
    head_size = feature_width // head_count
    factor = head_size ** (-0.5)
    query_heads = queries.reshape(row_count, head_count, head_size)
    key_heads = key_rows.reshape(-1, head_count, head_size)
    value_heads = value_rows.reshape(-1, head_count, head_size)
    grad_heads = grad_rows.reshape(row_count, head_count, head_size)
    scores = jnp.einsum("qhd,khd->hqk", query_heads, key_heads, preferred_element_type=jnp.float32)
    weights = jnp.exp(scores * factor - saved_sums[:, :, None]) * retain
    d_values = jnp.einsum(
        "hqk,qhd->khd", weights.astype(jnp.bfloat16), grad_heads, preferred_element_type=jnp.float32
    )
    d_weights = jnp.einsum(
        "qhd,khd->hqk", grad_heads, value_heads, preferred_element_type=jnp.float32
    )
    d_scores = (weights * (d_weights - saved_delta[:, :, None])).astype(jnp.bfloat16)
    d_query = (
        jnp.einsum("hqk,khd->qhd", d_scores, key_heads, preferred_element_type=jnp.float32) * factor
    )
    d_keys = (
        jnp.einsum("hqk,qhd->khd", d_scores, query_heads, preferred_element_type=jnp.float32)
        * factor
    )
    return (
        d_query.reshape(row_count, feature_width),
        d_keys.reshape(-1, feature_width),
        d_values.reshape(-1, feature_width),
    )


def on_device(
    query_tiles,
    key_tiles,
    value_tiles,
    grad_tiles,
    log_sums,
    row_delta,
    text_keys,
    text_values,
    touch_list,
):
    queries = query_tiles[0, 0]
    key_rows = key_tiles[0, 0]
    value_rows = value_tiles[0, 0]
    grad_rows = grad_tiles[0, 0]
    sums_now = log_sums[0, 0]
    delta_now = row_delta[0, 0]
    row_count, feature_width = queries.shape
    text_both = lax.all_gather(jnp.stack([text_keys, text_values]), "space", axis=1, tiled=True)
    text_count = text_both.shape[1]
    touched = jnp.any(
        touch_list[0, 0][:, None] == jnp.arange(text_count, dtype=jnp.int32)[None, :], axis=0
    ).astype(jnp.float32)
    time_index = lax.axis_index("tm")
    time_count = lax.axis_size("tm")
    retain_before = (time_index >= 1).astype(jnp.float32)
    retain_after = (time_index + 1 < time_count).astype(jnp.float32)
    local = block_grads(
        queries, key_rows, value_rows, grad_rows, sums_now, delta_now, jnp.float32(1.0)
    )
    textual = block_grads(
        queries, text_both[0], text_both[1], grad_rows, sums_now, delta_now, touched
    )
    widened = extended(jnp.stack([key_rows, value_rows]), (("tm", 1),), row_count)
    below_part = block_grads(
        queries,
        widened[0, :row_count],
        widened[1, :row_count],
        grad_rows,
        sums_now,
        delta_now,
        retain_before,
    )
    above_part = block_grads(
        queries,
        widened[0, 2 * row_count :],
        widened[1, 2 * row_count :],
        grad_rows,
        sums_now,
        delta_now,
        retain_after,
    )
    from_above = from_behind(
        jnp.stack([below_part[1], below_part[2]]).astype(jnp.bfloat16), "tm", -1
    )
    from_below = from_behind(
        jnp.stack([above_part[1], above_part[2]]).astype(jnp.bfloat16), "tm", 1
    )
    query_sum = (
        rounded(local[0]) + rounded(below_part[0]) + rounded(above_part[0]) + rounded(textual[0])
    )
    key_sum = (
        rounded(local[1]) + from_above[0].astype(jnp.float32) + from_below[0].astype(jnp.float32)
    )
    value_sum = (
        rounded(local[2]) + from_above[1].astype(jnp.float32) + from_below[1].astype(jnp.float32)
    )
    text_terms = jnp.stack([textual[1], textual[2]])
    shared = lax.psum_scatter(text_terms, "space", scatter_dimension=1, tiled=True)
    summed = lax.psum(shared, "tm")
    text_result = summed.astype(jnp.bfloat16)
    return (
        query_sum.astype(jnp.bfloat16)[None, None],
        key_sum.astype(jnp.bfloat16)[None, None],
        value_sum.astype(jnp.bfloat16)[None, None],
        text_result[0],
        text_result[1],
    )


def solution(mesh):
    return jax.shard_map(
        on_device,
        mesh=mesh,
        in_specs=(
            P("tm", "space", None, None),
            P("tm", "space", None, None),
            P("tm", "space", None, None),
            P("tm", "space", None, None),
            P("tm", "space", None, None),
            P("tm", "space", None, None),
            P("space", None),
            P("space", None),
            P("tm", "space", None),
        ),
        out_specs=(
            P("tm", "space", None, None),
            P("tm", "space", None, None),
            P("tm", "space", None, None),
            P("space", None),
            P("space", None),
        ),
        check_vma=False,
    )
```

profile of v0, /device:TPU:1, one launch (start us, length us, event | category | flops | bytes accessed | tf_op | source)
XLA Modules:
  0.0 298.5 jit_solution(15602903051137748115)
XLA Ops:
  12.3 5.3 %collective-permute-start.1 = (bf16[2,256,1536]{1,2,0:T(8,128)(2,1)}, bf16[2,256,1536]{1,2,0:T(8,128)(2,1)}, u32[]{:S(2)}, u32[]{:S(2)}) collective-permute-start(bf16[2,256,1536]{1,2,0:T(8,128)(2,1)} %pad_maximum_fusion.1), channel_id=1, source_target_pairs={{8,0},{16,8},{24,16},{32,24},{40,32},{48,40},{56,48},{64,56},{72,6... | collective-permute-start | bytes 4718600 | tf_op jit(solution)/shard_map/ppermute | solution.py:15
  17.6 1.9 collective-permute-start
  24.2 1.7 fusion.25
  25.9 34.1 %all-gather.2.cloned.1.call-done = bf16[2,256,1536]{2,0,1:T(2,128)(2,1)} async-done(((bf16[2,32,1536]{2,0,1:T(2,128)(2,1)}), bf16[2,256,1536]{2,0,1:T(2,128)(2,1)}) %all-gather.2.cloned.1.call-update) | async-done | bytes 1572880 | tf_op jit(solution)/shard_map/all_gather | solution.py:80
  60.0 5.8 %fusion.44 = (bf16[1,256,1536]{2,0,1:T(2,128)(2,1)}, bf16[1,256,1536]{2,0,1:T(2,128)(2,1)}) fusion(bf16[2,256,1536]{2,0,1:T(2,128)(2,1)} %all-gather.2.cloned.1.call-done), kind=kLoop, calls=%fused_computation.69 | loop fusion | bytes 3145728 | tf_op jit(solution)/shard_map/slice | solution.py:93
  65.8 4.6 %copy.176 = bf16[1,256,1536]{1,2,0:T(8,128)(2,1)} copy(bf16[1,256,1536]{2,0,1:T(2,128)(2,1)} %get-tuple-element.12) | data formatting | bytes 1572864
  70.5 3.4 %fusion.48 = f32[12,256,256]{2,1,0:T(8,128)} fusion(bf16[256,12,128]{0,2,1:T(8,128)(2,1)} %bitcast.142, bf16[256,12,128]{0,2,1:T(8,128)(2,1)S(1)} %bitcast.123), kind=kOutput, calls=%fused_computation.73 | convolution fusion | flops 201326592 | bytes 4718592 | tf_op jit(solution)/shard_map/qhd,khd->hqk/dot_general | solution.py:39
  73.9 4.6 %copy.177 = bf16[1,256,1536]{1,2,0:T(8,128)(2,1)} copy(bf16[1,256,1536]{2,0,1:T(2,128)(2,1)} %get-tuple-element.11) | data formatting | bytes 1572864
  78.5 3.9 %fusion.4 = f32[12,256,128]{1,2,0:T(8,128)} fusion(bf16[256,12,128]{0,2,1:T(8,128)(2,1)S(1)} %bitcast.131, f32[12,256,256]{2,1,0:T(8,128)} %fusion.48, f32[256]{0:T(256)S(1)} %convert_element_type.164, f32[12,256]{1,0:T(8,128)S(1)} %get-tuple-element.16), kind=kOutput, calls=%fused_computation.13 | convolution fusion | flops 204472320 | bytes 5518336 | tf_op jit(solution)/shard_map/hqk,qhd->khd/dot_general | solution.py:41
  82.4 3.0 %copy.157 = f32[1,256,1536]{2,1,0:T(8,128)} copy(f32[1,256,1536]{1,2,0:T(8,128)} %bitcast.148) | data formatting | bytes 3145728 | tf_op jit(solution)/shard_map/stack;reshape | solution.py:129
  85.4 3.2 %multiply_convert_fusion = bf16[12,256,256]{2,1,0:T(8,128)(2,1)S(1)} fusion(f32[12,256,256]{2,1,0:T(8,128)} %fusion.48, bf16[256,12,128]{0,2,1:T(8,128)(2,1)} %bitcast.160, bf16[256,12,128]{0,2,1:T(8,128)(2,1)S(1)} %bitcast.132, f32[256]{0:T(256)S(1)} %convert_element_type.164, f32[12,256]{1,0:T(8,128)S(1)} %get-tuple-element.15, ...), kind=kOutput, calls=%fused_computation.1 | convolution fusion | flops 206045184 | bytes 6317056 | tf_op jit(solution)/shard_map/qhd,khd->hqk/dot_general | solution.py:44
  88.7 1.8 convolution_multiply_fusion
  90.5 3.0 %copy.156 = f32[1,256,1536]{2,1,0:T(8,128)} copy(f32[1,256,1536]{1,2,0:T(8,128)} %bitcast.149) | data formatting | bytes 3145728 | tf_op jit(solution)/shard_map/stack;reshape | solution.py:129
  93.5 3.7 %pad_maximum_fusion = f32[2,256,1536]{2,1,0:T(8,128)} fusion(f32[1,256,1536]{2,1,0:T(8,128)} %copy.157, f32[1,256,1536]{2,1,0:T(8,128)} %copy.156), kind=kLoop, calls=%fused_computation | loop fusion | flops 786432 | bytes 6291456 | tf_op jit(solution)/shard_map/stack | solution.py:129
  97.3 2.4 fusion.42
  101.1 1.9 fusion.28
  103.1 2.3 copy.152
  105.3 3.2 %multiply_convert_fusion.2 = bf16[12,256,256]{2,1,0:T(8,128)(2,1)S(1)} fusion(f32[12,256,256]{2,1,0:T(8,128)} %copy-done.7, bf16[256,12,128]{0,2,1:T(8,128)(2,1)} %bitcast.152, bf16[256,12,128]{0,2,1:T(8,128)(2,1)S(1)} %bitcast.134, f32[12,256]{1,0:T(8,128)S(1)} %get-tuple-element.15, f32[]{:T(128)S(6)} %convert_element_type.152, ...), kind=kOutput, calls=%fused_computation.3 | convolution fusion | flops 206045184 | bytes 6316036 | tf_op jit(solution)/shard_map/qhd,khd->hqk/dot_general | solution.py:44
  110.0 2.3 copy.151
  112.3 2.7 pad_maximum_fusion.2
  115.0 6.3 %collective-permute-start.2 = (bf16[2,256,1536]{2,1,0:T(8,128)(2,1)}, bf16[2,256,1536]{2,1,0:T(8,128)(2,1)}, u32[]{:S(2)}, u32[]{:S(2)}) collective-permute-start(bf16[2,256,1536]{2,1,0:T(8,128)(2,1)} %pad_maximum_fusion.2), channel_id=1, source_target_pairs={{8,0},{16,8},{24,16},{32,24},{40,32},{48,40},{56,48},{64,56},{72,6... | collective-permute-start | bytes 4718600 | tf_op jit(solution)/shard_map/ppermute | solution.py:23
  121.4 2.4 fusion.43
  125.3 1.9 fusion.31
  127.2 2.3 copy.154
  129.5 3.2 %multiply_convert_fusion.1 = bf16[12,256,256]{2,1,0:T(8,128)(2,1)S(1)} fusion(f32[12,256,256]{2,1,0:T(8,128)} %copy-done.6, bf16[256,12,128]{0,2,1:T(8,128)(2,1)} %bitcast.151, bf16[256,12,128]{0,2,1:T(8,128)(2,1)S(1)} %bitcast.136, f32[]{:T(128)S(6)} %convert_element_type.158, f32[12,256]{1,0:T(8,128)S(1)} %get-tuple-element.15, ...), kind=kOutput, calls=%fused_computation.2 | convolution fusion | flops 206045184 | bytes 6316036 | tf_op jit(solution)/shard_map/qhd,khd->hqk/dot_general | solution.py:44
  137.0 2.0 collective-permute-start.3
  141.8 2.4 copy.129
  146.7 2.4 copy.136
  150.4 2.4 copy.141
  154.5 2.5 fusion.34
  157.1 3.6 %fusion.36 = (bf16[1,1,256,1536]{3,2,1,0:T(8,128)(2,1)}, bf16[1,1,256,1536]{3,2,1,0:T(8,128)(2,1)}) fusion(bf16[256,1536]{1,0:T(8,128)(2,1)S(1)} %copy-done.18, bf16[2,256,1536]{2,1,0:T(8,128)(2,1)} %collective-permute-done.3, bf16[2,256,1536]{2,1,0:T(8,128)(2,1)} %collective-permute-done.2, bf16[256,1536]{1,0:T(8,128)(2,1)S(1)} %copy-done.19), kind=kLoop, calls=%fused_computation.51 | loop fusion | flops 4718592 | bytes 6291456 | tf_op jit(solution)/shard_map/broadcast_in_dim | solution.py:136
  160.7 130.3 %all-reduce.1 = bf16[2,32,1536]{2,1,0:T(8,128)(2,1)S(1)} all-reduce(f32[2,32,1536]{2,1,0:T(8,128)} %reduce-scatter.2.cloned.1.call-done), channel_id=1, replica_groups=mesh['tm'=32,'space'=8] {'tm'}, use_global_device_ids=true, to_apply=%region_2.0 | all-reduce | flops 98304 | bytes 589824 | tf_op jit(solution)/shard_map/psum | solution.py:131
  (96 shorter events, 27.4 us)
Async XLA Ops:
  7.2 3.4 %copy-start.24 = (bf16[1,1,256,1536]{3,2,1,0:T(8,128)(2,1)S(1)}, bf16[1,1,256,1536]{3,2,1,0:T(8,128)(2,1)}, u32[]{:S(2)}) copy-start(bf16[1,1,256,1536]{3,2,1,0:T(8,128)(2,1)} %param.11) | copy-start | bytes 2359300
  7.2 52.9 %all-gather.2.cloned.1.call-start = ((), (), s32[]{:S(2)}) async-start(), calls=%async_computation.1 | async-start | bytes 1769472 | tf_op jit(solution)/shard_map/all_gather | solution.py:80
  9.2 151.5 %reduce-scatter.2.cloned.1.call-start = ((), (), s32[]{:S(2)}) async-start(), calls=%async_computation.2 | async-start | bytes 3538944 | tf_op jit(solution)/shard_map/reduce_scatter | solution.py:130
  10.6 9.8 %copy-start.8 = (bf16[1,1,256,1536]{2,3,1,0:T(8,128)(2,1)}, bf16[1,1,256,1536]{2,3,1,0:T(8,128)(2,1)S(1)}, u32[]{:S(2)}) copy-start(bf16[1,1,256,1536]{2,3,1,0:T(8,128)(2,1)S(1)} %copy.122) | copy-start | bytes 2359300
  10.9 1.4 copy-start.10
  10.9 8.6 %copy-start.29 = (s32[1,1,128]{2,1,0:T(1,128)S(1)}, s32[1,1,128]{2,1,0:T(1,128)}, u32[]{:S(2)}) copy-start(s32[1,1,128]{2,1,0:T(1,128)} %param.17) | copy-start | bytes 1540
  10.9 8.8 %copy-start.25 = (bf16[1,1,256,1536]{3,2,1,0:T(8,128)(2,1)S(1)}, bf16[1,1,256,1536]{3,2,1,0:T(8,128)(2,1)}, u32[]{:S(2)}) copy-start(bf16[1,1,256,1536]{3,2,1,0:T(8,128)(2,1)} %param.9) | copy-start | bytes 2359300
  12.3 7.7 %copy-start.26 = (bf16[1,1,256,1536]{3,2,1,0:T(8,128)(2,1)S(1)}, bf16[1,1,256,1536]{3,2,1,0:T(8,128)(2,1)}, u32[]{:S(2)}) copy-start(bf16[1,1,256,1536]{3,2,1,0:T(8,128)(2,1)} %param.12) | copy-start | bytes 2359300
  12.3 109.0 %collective-permute-start.1 = (bf16[2,256,1536]{1,2,0:T(8,128)(2,1)}, bf16[2,256,1536]{1,2,0:T(8,128)(2,1)}, u32[]{:S(2)}, u32[]{:S(2)}) collective-permute-start(bf16[2,256,1536]{1,2,0:T(8,128)(2,1)} %pad_maximum_fusion.1), channel_id=1, source_target_pairs={{8,0},{16,8},{24,16},{32,24},{40,32},{48,40},{56,48},{64,56},{72,6... | collective-permute-start | bytes 4718600 | tf_op jit(solution)/shard_map/ppermute | solution.py:15
  17.6 79.6 %collective-permute-start = (bf16[2,256,1536]{1,2,0:T(8,128)(2,1)}, bf16[2,256,1536]{1,2,0:T(8,128)(2,1)}, u32[]{:S(2)}, u32[]{:S(2)}) collective-permute-start(bf16[2,256,1536]{1,2,0:T(8,128)(2,1)} %pad_maximum_fusion.1), channel_id=1, source_target_pairs={{0,8},{8,16},{16,24},{24,32},{32,40},{40,48},{48,56},{56,64},{64,7... | collective-permute-start | bytes 4718600 | tf_op jit(solution)/shard_map/ppermute | solution.py:12
  20.4 1.1 copy-start.11
  88.7 1.8 copy-start.4
  101.1 1.9 copy-start.7
  108.5 1.5 copy-start
  115.0 42.1 %collective-permute-start.2 = (bf16[2,256,1536]{2,1,0:T(8,128)(2,1)}, bf16[2,256,1536]{2,1,0:T(8,128)(2,1)}, u32[]{:S(2)}, u32[]{:S(2)}) collective-permute-start(bf16[2,256,1536]{2,1,0:T(8,128)(2,1)} %pad_maximum_fusion.2), channel_id=1, source_target_pairs={{8,0},{16,8},{24,16},{32,24},{40,32},{48,40},{56,48},{64,56},{72,6... | collective-permute-start | bytes 4718600 | tf_op jit(solution)/shard_map/ppermute | solution.py:23
  125.2 1.9 copy-start.6
  132.7 1.5 copy-start.2
  134.2 1.5 copy-start.21
  135.7 3.4 %copy-start.9 = (bf16[1,1,256,1536]{2,3,1,0:T(8,128)(2,1)S(1)}, bf16[1,1,256,1536]{2,3,1,0:T(8,128)(2,1)}, u32[]{:S(2)}) copy-start(bf16[1,1,256,1536]{2,3,1,0:T(8,128)(2,1)} %copy-done.8) | copy-start | bytes 2359300
  137.0 3.6 %copy-start.17 = (bf16[12,256,128]{1,2,0:T(8,128)(2,1)S(1)}, bf16[12,256,128]{1,2,0:T(8,128)(2,1)}, u32[]{:S(2)}) copy-start(bf16[12,256,128]{1,2,0:T(8,128)(2,1)} %fusion.25) | copy-start | bytes 2359300
  137.0 20.0 %collective-permute-start.3 = (bf16[2,256,1536]{2,1,0:T(8,128)(2,1)}, bf16[2,256,1536]{2,1,0:T(8,128)(2,1)}, u32[]{:S(2)}, u32[]{:S(2)}) collective-permute-start(bf16[2,256,1536]{2,1,0:T(8,128)(2,1)} %pad_maximum_fusion.3), channel_id=1, source_target_pairs={{0,8},{8,16},{16,24},{24,32},{32,40},{40,48},{48,56},{56,64},{64,7... | collective-permute-start | bytes 4718600 | tf_op jit(solution)/shard_map/ppermute | solution.py:23
  140.6 3.6 %copy-start.20 = (bf16[12,256,128]{1,2,0:T(8,128)(2,1)S(1)}, bf16[12,256,128]{1,2,0:T(8,128)(2,1)}, u32[]{:S(2)}) copy-start(bf16[12,256,128]{1,2,0:T(8,128)(2,1)} %multiply_convert_fusion.6) | copy-start | bytes 2359300
  141.8 3.6 %copy-start.1 = (bf16[12,256,256]{2,1,0:T(8,128)(2,1)S(1)}, bf16[12,256,256]{2,1,0:T(8,128)(2,1)}, u32[]{:S(2)}) copy-start(bf16[12,256,256]{2,1,0:T(8,128)(2,1)} %copy-done) | copy-start | bytes 4718596
  141.8 3.6 %copy-start.14 = (bf16[1,256,1536]{1,2,0:T(8,128)(2,1)S(1)}, bf16[1,256,1536]{1,2,0:T(8,128)(2,1)}, u32[]{:S(2)}) copy-start(bf16[1,256,1536]{1,2,0:T(8,128)(2,1)} %copy-done.13) | copy-start | bytes 2359300
  145.4 3.7 %copy-start.16 = (bf16[1,256,1536]{1,2,0:T(8,128)(2,1)S(1)}, bf16[1,256,1536]{1,2,0:T(8,128)(2,1)}, u32[]{:S(2)}) copy-start(bf16[1,256,1536]{1,2,0:T(8,128)(2,1)} %copy-done.15) | copy-start | bytes 2359300
  146.7 2.4 copy-start.3
  149.1 3.7 %copy-start.12 = (bf16[1,256,1536]{1,2,0:T(8,128)(2,1)S(1)}, bf16[1,256,1536]{1,2,0:T(8,128)(2,1)}, u32[]{:S(2)}) copy-start(bf16[1,256,1536]{1,2,0:T(8,128)(2,1)} %copy.176) | copy-start | bytes 2359300
  150.4 2.4 copy-start.5
  153.2 1.1 copy-start.22
  153.2 1.4 copy-start.23
  154.5 2.5 copy-start.18
  154.5 2.5 copy-start.19
  (4 other events, 3.2 us)
Sparse Core Ops, SparseCore 0:
  10.4 49.6 all-gather.1
  97.4 45.8 reduce-scatter.1
where the time goes:
time: 303 us; the launch traced here: 298 us
  blocking collectives  130 us (43%)
  local copies, waits for them, and re-layouts  51.4 us (17%)
  matrix products  36.2 us (12%)
  waiting for transfers between devices  34.2 us (11%)
  other arithmetic  16.3 us (5%)
  starting transfers between devices  15.7 us (5%)
  between operations  14.4 us (5%)
    psum x1, blocking collectives, on_device(): summed = lax.psum(shared, 'tm')  130 us
    all_gather x1, waiting for transfers between devices, on_device(): lax.all_gather(jnp.stack([text_keys, text_values]), 'space', axis=1, tile...  34.1 us
    unnamed x67, local copies, waits for them, and re-layouts  15.1 us
    dot_general x4, matrix products, block_grads(): jnp.einsum('qhd,khd->hqk', grad_heads, value_heads, preferred_element_typ...  10.9 us
    optimization_barrier x6, local copies, waits for them, and re-layouts, rounded(): lax.optimization_barrier(values_in.astype(jnp.bfloat16)).astype(jnp.float32)  9.87 us
    dot_general x4, matrix products, block_grads(): jnp.einsum('hqk,qhd->khd', weights.astype(jnp.bfloat16), grad_heads, pref...  9.38 us
    ppermute x2, starting transfers between devices, from_behind(): lax.ppermute(value, axis, [(source, source + steps) for source in range(l...  8.38 us
    dot_general x4, matrix products, block_grads(): jnp.einsum('hqk,qhd->khd', d_scores, query_heads, preferred_element_type=...  6.17 us
  transfers between devices with their start and end apart: 6, of which 1 were waited for; matrix products, arithmetic and copies ran while one was open for 33% of the time, Pallas kernels for 0%

commit v1 on v0

v1 whole, which is shorter than its diff:
```python
import functools
import math

import jax
import jax.numpy as jnp
from jax import lax
from jax.experimental import pallas as pl
from jax.experimental.pallas import tpu as pltpu
from jax.sharding import PartitionSpec as P

MESH = pl.DeviceIdType.MESH
BF16 = jnp.bfloat16
F32 = jnp.float32
HEADS = 12
HEAD = 128
ROWS = 256
WIDTH = HEADS * HEAD
TEXT = 256
TOUCH = 128
SHARD = 32
FACTOR = HEAD**-0.5
LOG2E = math.log2(math.e)
AT_TEXT, AT_PAIR, AT_DQ = 5, 8, 6


def rnd(value):
    return value.astype(BF16).astype(F32)


def dot_nt(a, b):
    return lax.dot_general(a, b, (((1,), (1,)), ((), ())), preferred_element_type=F32)


def dot_nn(a, b):
    return lax.dot_general(a, b, (((1,), (0,)), ((), ())), preferred_element_type=F32)


def pair(queries, grads, sums_row, delta_row, keys, keys_t, values):
    scores = dot_nt(keys, queries)
    weights = jnp.exp2(scores * (FACTOR * LOG2E) - sums_row * LOG2E)
    d_values = dot_nn(weights.astype(BF16), grads)
    d_weights = dot_nt(values, grads)
    d_scores = (weights * (d_weights - delta_row)).astype(BF16)
    d_keys = dot_nn(d_scores, queries) * FACTOR
    d_query = (dot_nn(keys_t, d_scores) * FACTOR).astype(BF16).T
    return d_query, d_keys, d_values


def kernel(
    q_hbm, k_hbm, v_hbm, g_hbm, sums_hbm, delta_hbm, tk_hbm, tv_hbm, touch_hbm,
    dq_out, dk_out, dv_out, tk_out, tv_out,
    tiles, sums, delta, keys_t, k_own, v_own, text, touch,
    dq_acc, dk_acc, dv_acc, dq_sent, dq_back, outs,
    text_f32, text_b16, text_pair, text_sum, plane, plane_sum, z_part, final, wide, text_done,
    load_sem, qg_send, qg_recv, st_send, st_recv, fast_send, fast_recv, dqf_sem, dqs_send, dqs_recv,
    gather_send, gather_recv, fwd_send, fwd_recv, pair_sem, plane_send, plane_recv,
    zr_send, zr_recv, zg_send, zg_recv, done_send, done_recv, out_sem,
):
    t = lax.axis_index("tm")
    s = lax.axis_index("space")
    core = t % 2
    z = (t // 2) % 8
    y_hi = t // 16
    x = s % 4
    y = y_hi * 2 + s // 4
    me = y * 4 + x
    fast = (t + 1 - 2 * core, s)
    slow_t = t - 1 + 2 * core
    has_slow = jnp.logical_and(slow_t >= 0, slow_t < 32)
    slow = (jnp.where(has_slow, slow_t, t), s)
    turn = (x - y + 3) % 4
    active = turn < 3
    my_head = jnp.where(active, 3 * y + turn, 0)

    def chip(place, core_at):
        py, px = place // 4, place % 4
        return (((py // 2) * 8 + z) * 2 + core_at, (py % 2) * 4 + px)

    def along_z(z_at):
        return ((y_hi * 8 + z_at) * 2 + core, s)

    def cols(h):
        return pl.ds(pl.multiple_of(h * HEAD, HEAD), HEAD)

    def rows_of(i, size):
        return pl.ds(pl.multiple_of(i * size, size), size)

    def remote(src, dst, send, recv, device):
        return pltpu.make_async_remote_copy(
            src_ref=src, dst_ref=dst, send_sem=send, recv_sem=recv, device_id=device, device_id_type=MESH
        )

    def loop(count, body):
        lax.fori_loop(0, count, lambda i, c: (body(i), c)[1], 0)

    loads = [
        pltpu.make_async_copy(src, dst, load_sem.at[i])
        for i, (src, dst) in enumerate(
            (
                (q_hbm, tiles.at[0, 0]), (k_hbm, k_own), (g_hbm, tiles.at[0, 1]), (v_hbm, v_own),
                (sums_hbm, sums.at[0]), (delta_hbm, delta.at[0]), (touch_hbm, touch),
                (tk_hbm, text.at[0, rows_of(s, SHARD)]), (tv_hbm, text.at[1, rows_of(s, SHARD)]),
            )
        )
    ]
    for load in loads:
        load.start()

    barrier = pltpu.get_barrier_semaphore()

    def greet_plane(i):
        @pl.when(i != me * 2 + core)
        def _():
            pl.semaphore_signal(barrier, 1, device_id=chip(i // 2, i % 2), device_id_type=MESH)

    def greet_z(i):
        @pl.when(i != z)
        def _():
            pl.semaphore_signal(barrier, 1, device_id=along_z(i), device_id_type=MESH)

    @pl.when(has_slow)
    def _():
        pl.semaphore_signal(barrier, 1, device_id=slow, device_id_type=MESH)

    loop(32, greet_plane)
    loop(8, greet_z)
    pl.semaphore_wait(barrier, 38 + has_slow.astype(jnp.int32))

    def slow_stats(i):
        src, dst = ((sums_hbm, sums.at[2]), (delta_hbm, delta.at[2]))[i]
        return remote(src, dst, st_send.at[i], st_recv.at[i], slow)

    def slow_tile(i, h):
        src = (q_hbm, g_hbm)[i]
        return remote(
            src.at[:, cols(h)], tiles.at[2, i, :, cols(h)], qg_send.at[i, h], qg_recv.at[i, h], slow
        )

    def fast_copy(i):
        src, dst = (
            (sums_hbm, sums.at[1]), (delta_hbm, delta.at[1]), (q_hbm, tiles.at[1, 0]), (g_hbm, tiles.at[1, 1]),
        )[i]
        return remote(src, dst, fast_send.at[i], fast_recv.at[i], fast)

    @pl.when(has_slow)
    def _():
        for i in range(2):
            slow_stats(i).start()

        def send(h):
            slow_tile(0, h).start()
            slow_tile(1, h).start()

        loop(HEADS, send)

    for i in range(4):
        fast_copy(i).start()

    for load in loads[6:]:
        load.wait()

    def gather(i, owner):
        part = text.at[core, rows_of(owner, SHARD)]
        return remote(part, part, gather_send.at[i], gather_recv.at[owner], (t, i))

    def forward(i):
        part = text.at[core, rows_of(i, SHARD)]
        return remote(part, part, fwd_send.at[i], fwd_recv.at[i], fast)

    def forwarded(i):
        part = text.at[1 - core, rows_of(i, SHARD)]
        return remote(part, part, fwd_send.at[i], fwd_recv.at[i], fast)

    def unless(i, own, body):
        @pl.when(i != own)
        def _():
            body()

    loop(8, lambda i: unless(i, s, lambda: gather(i, s).start()))
    for load in loads[:6]:
        load.wait()

    def own_head(h):
        keys = k_own[:, cols(h)]
        turned = keys.T
        keys_t[h] = turned
        dq, dk, dv = pair(
            tiles[0, 0, :, cols(h)], tiles[0, 1, :, cols(h)], sums[0, pl.ds(h, 1), :], delta[0, pl.ds(h, 1), :],
            keys, turned, v_own[:, cols(h)],
        )
        dq_acc[:, cols(h)] = dq.astype(F32)
        dk_acc[:, cols(h)] = rnd(dk)
        dv_acc[:, cols(h)] = rnd(dv)

    loop(HEADS, own_head)

    def near_head(h, slot):
        dq, dk, dv = pair(
            tiles[slot, 0, :, cols(h)], tiles[slot, 1, :, cols(h)],
            sums[slot, pl.ds(h, 1), :], delta[slot, pl.ds(h, 1), :],
            k_own[:, cols(h)], keys_t[h], v_own[:, cols(h)],
        )
        dq_sent[slot - 1, :, cols(h)] = dq
        dk_acc[:, cols(h)] += rnd(dk)
        dv_acc[:, cols(h)] += rnd(dv)

    for i in range(4):
        fast_copy(i).wait_recv()
    loop(HEADS, lambda h: near_head(h, 1))
    dq_fast = remote(dq_sent.at[0], dq_back.at[0], dqf_sem.at[0], dqf_sem.at[1], fast)
    dq_fast.start()

    def hand_over(i):
        gather(i, i).wait_recv()
        forward(i).start()

    loop(8, lambda i: unless(i, s, lambda: hand_over(i)))

    pair_copy = remote(text_b16.at[1 - core], text_pair, pair_sem.at[0], pair_sem.at[1], fast)

    def token_rows():
        token = lax.broadcasted_iota(jnp.int32, (TEXT, TOUCH), 0)
        return jnp.where(token == touch[...], 1.0, 0.0).astype(F32)

    def text_block():
        loop(8, lambda i: unless(i, s, lambda: forwarded(i).wait_recv()))
        pick = token_rows().T.astype(BF16)

        def head(h):
            keys = dot_nn(pick, text[0, :, cols(h)]).astype(BF16)
            values = dot_nn(pick, text[1, :, cols(h)]).astype(BF16)
            dq, dk, dv = pair(
                tiles[0, 0, :, cols(h)], tiles[0, 1, :, cols(h)],
                sums[0, pl.ds(h, 1), :], delta[0, pl.ds(h, 1), :],
                keys, keys.T, values,
            )
            dq_acc[:, cols(h)] += dq.astype(F32)
            text_f32[0, :, cols(h)] = dk
            text_f32[1, :, cols(h)] = dv
            text_b16[0, :, cols(h)] = dk.astype(BF16)
            text_b16[1, :, cols(h)] = dv.astype(BF16)

        loop(HEADS, head)
        pair_copy.start()

    def head_place(h):
        py = h // 3
        return py * 4 + (py + 1 + h % 3) % 4

    def to_plane(h, src):
        return remote(
            text_sum.at[:, cols(h)], plane.at[src], plane_send.at[h], plane_recv.at[src],
            chip(head_place(h), core),
        )

    def pair_sum():
        pair_copy.wait_recv()

        def head(h):
            text_sum[:, cols(h)] = (text_f32[core, :, cols(h)] + text_pair[:, cols(h)].astype(F32)).astype(BF16)

        loop(HEADS, head)
        loop(HEADS, lambda h: unless(head_place(h), me, lambda: to_plane(h, me).start()))

    def dq_slow(h):
        return remote(
            dq_sent.at[1, :, cols(h)], dq_back.at[1, :, cols(h)], dqs_send.at[h], dqs_recv.at[h], slow
        )

    @pl.when(has_slow)
    def _():
        for i in range(2):
            slow_stats(i).wait_recv()

    def slow_head(h):
        pl.when(h == AT_TEXT)(text_block)
        pl.when(h == AT_PAIR)(pair_sum)

        @pl.when(has_slow)
        def _():
            slow_tile(0, h).wait_recv()
            slow_tile(1, h).wait_recv()
            near_head(h, 2)

            @pl.when(h >= AT_DQ)
            def _():
                dq_slow(2 * (h - AT_DQ)).start()
                dq_slow(2 * (h - AT_DQ) + 1).start()

        outs[1, :, cols(h)] = dk_acc[:, cols(h)].astype(BF16)
        outs[2, :, cols(h)] = dv_acc[:, cols(h)].astype(BF16)

    loop(HEADS, slow_head)
    out_copies = [
        pltpu.make_async_copy(outs.at[1], dk_out, out_sem.at[1]),
        pltpu.make_async_copy(outs.at[2], dv_out, out_sem.at[2]),
    ]
    for copy in out_copies:
        copy.start()

    def z_reduce(i, src):
        return remote(
            plane_sum.at[rows_of(i, 16)], z_part.at[src], zr_send.at[i], zr_recv.at[src], along_z(i)
        )

    def z_spread(i, src):
        part = final.at[rows_of(src, 16)]
        return remote(part, part, zg_send.at[i], zg_recv.at[src], along_z(i))

    def deliver(i, head, core_at):
        place = i // 2
        owner = (place // 4 % 2) * 4 + place % 4
        return remote(
            wide.at[rows_of(owner, SHARD)], text_done.at[core_at, :, cols(head)],
            done_send.at[i], done_recv.at[core_at * HEADS + head], chip(place, i % 2),
        )

    @pl.when(active)
    def _():
        plane[me] = text_sum[:, cols(my_head)]
        loop(16, lambda p: unless(p, me, lambda: to_plane(my_head, p).wait_recv()))
        total = plane[0].astype(F32)
        for p in range(1, 16):
            total = total + plane[p].astype(F32)
        plane_sum[...] = total.astype(BF16)
        loop(8, lambda i: unless(i, z, lambda: z_reduce(i, z).start()))
        z_part[z] = plane_sum[rows_of(z, 16), :]
        loop(8, lambda i: unless(i, z, lambda: z_reduce(z, i).wait_recv()))
        total = z_part[0].astype(F32)
        for p in range(1, 8):
            total = total + z_part[p].astype(F32)
        final[rows_of(z, 16), :] = total.astype(BF16)
        loop(8, lambda i: unless(i, z, lambda: z_spread(i, z).start()))
        loop(8, lambda i: unless(i, z, lambda: z_spread(z, i).wait_recv()))
        wide[...] = dot_nn(token_rows().astype(BF16), final[...]).astype(BF16)
        loop(32, lambda i: unless(i, me * 2 + core, lambda: deliver(i, my_head, core).start()))
        text_done[core, :, cols(my_head)] = wide[rows_of(s, SHARD), :]

    dq_fast.wait_recv()

    def finish(h):
        @pl.when(has_slow)
        def _():
            dq_slow(h).wait_recv()

        both = dq_acc[:, cols(h)] + dq_back[0, :, cols(h)].astype(F32)

        @pl.when(has_slow)
        def _():
            outs[0, :, cols(h)] = (both + dq_back[1, :, cols(h)].astype(F32)).astype(BF16)

        @pl.when(jnp.logical_not(has_slow))
        def _():
            outs[0, :, cols(h)] = both.astype(BF16)

    loop(HEADS, finish)
    dq_copy = pltpu.make_async_copy(outs.at[0], dq_out, out_sem.at[0])
    dq_copy.start()

    def done_from(i):
        head, core_at = i % HEADS, i // HEADS
        own = jnp.logical_and(jnp.logical_and(active, head == my_head), core_at == core)

        @pl.when(jnp.logical_not(own))
        def _():
            deliver(me * 2 + core, head, core_at).wait_recv()

    loop(2 * HEADS, done_from)
    text_copies = [
        pltpu.make_async_copy(text_done.at[0], tk_out, out_sem.at[3]),
        pltpu.make_async_copy(text_done.at[1], tv_out, out_sem.at[4]),
    ]
    for copy in text_copies:
        copy.start()

    for i in range(4):
        fast_copy(i).wait_send()
    dq_fast.wait_send()
    pair_copy.wait_send()
    loop(8, lambda i: unless(i, s, lambda: (gather(i, s).wait_send(), forward(i).wait_send())))
    loop(HEADS, lambda h: unless(head_place(h), me, lambda: to_plane(h, me).wait_send()))

    @pl.when(has_slow)
    def _():
        for i in range(2):
            slow_stats(i).wait_send()

        def sent(h):
            slow_tile(0, h).wait_send()
            slow_tile(1, h).wait_send()
            dq_slow(h).wait_send()

        loop(HEADS, sent)

    @pl.when(active)
    def _():
        loop(8, lambda i: unless(i, z, lambda: (z_reduce(i, z).wait_send(), z_spread(i, z).wait_send())))
        loop(32, lambda i: unless(i, me * 2 + core, lambda: deliver(i, my_head, core).wait_send()))

    for copy in out_copies + text_copies + [dq_copy]:
        copy.wait()


def on_device(query_tiles, key_tiles, value_tiles, grad_tiles, log_sums, row_delta, text_keys, text_values, touch_list):
    tile = jax.ShapeDtypeStruct((ROWS, WIDTH), BF16)
    shard = jax.ShapeDtypeStruct((SHARD, WIDTH), BF16)
    dma = pltpu.SemaphoreType.DMA
    dq, dk, dv, tk, tv = pl.pallas_call(
        kernel,
        out_shape=(tile, tile, tile, shard, shard),
        in_specs=[pl.BlockSpec(memory_space=pl.ANY)] * 9,
        out_specs=[pl.BlockSpec(memory_space=pl.ANY)] * 5,
        scratch_shapes=[
            pltpu.VMEM((3, 2, ROWS, WIDTH), BF16),
            pltpu.VMEM((3, HEADS, ROWS), F32),
            pltpu.VMEM((3, HEADS, ROWS), F32),
            pltpu.VMEM((HEADS, HEAD, ROWS), BF16),
            pltpu.VMEM((ROWS, WIDTH), BF16),
            pltpu.VMEM((ROWS, WIDTH), BF16),
            pltpu.VMEM((2, TEXT, WIDTH), BF16),
            pltpu.VMEM((1, TOUCH), jnp.int32),
            pltpu.VMEM((ROWS, WIDTH), F32),
            pltpu.VMEM((ROWS, WIDTH), F32),
            pltpu.VMEM((ROWS, WIDTH), F32),
            pltpu.VMEM((2, ROWS, WIDTH), BF16),
            pltpu.VMEM((2, ROWS, WIDTH), BF16),
            pltpu.VMEM((3, ROWS, WIDTH), BF16),
            pltpu.VMEM((2, TOUCH, WIDTH), F32),
            pltpu.VMEM((2, TOUCH, WIDTH), BF16),
            pltpu.VMEM((TOUCH, WIDTH), BF16),
            pltpu.VMEM((TOUCH, WIDTH), BF16),
            pltpu.VMEM((16, TOUCH, HEAD), BF16),
            pltpu.VMEM((TOUCH, HEAD), BF16),
            pltpu.VMEM((8, 16, HEAD), BF16),
            pltpu.VMEM((TOUCH, HEAD), BF16),
            pltpu.VMEM((TEXT, HEAD), BF16),
            pltpu.VMEM((2, SHARD, WIDTH), BF16),
            dma((9,)),
            dma((2, HEADS)), dma((2, HEADS)),
            dma((2,)), dma((2,)),
            dma((4,)), dma((4,)),
            dma((2,)),
            dma((HEADS,)), dma((HEADS,)),
            dma((8,)), dma((8,)),
            dma((8,)), dma((8,)),
            dma((2,)),
            dma((HEADS,)), dma((16,)),
            dma((8,)), dma((8,)),
            dma((8,)), dma((8,)),
            dma((32,)), dma((2 * HEADS,)),
            dma((5,)),
        ],
        compiler_params=pltpu.CompilerParams(
            collective_id=0, has_side_effects=True, vmem_limit_bytes=60 << 20
        ),
    )(
        query_tiles[0, 0], key_tiles[0, 0], value_tiles[0, 0], grad_tiles[0, 0], log_sums[0, 0], row_delta[0, 0],
        text_keys, text_values, touch_list[0],
    )
    return dq[None, None], dk[None, None], dv[None, None], tk, tv


def solution(mesh):
    tile = P("tm", "space", None, None)
    return jax.shard_map(
        on_device,
        mesh=mesh,
        in_specs=(tile,) * 6 + (P("space", None), P("space", None), P("tm", "space", None)),
        out_specs=(tile, tile, tile, P("space", None), P("space", None)),
        check_vma=False,
    )
```

time: 303 us -> 85.4 us (0.28); the launches traced: 298 us -> 85.1 us
  blocking collectives: 130 us -> 0 us
  Pallas kernels: 0 us -> 77 us
  local copies, waits for them, and re-layouts: 51.4 us -> 7.42 us
  matrix products: 36.2 us -> 0 us
  waiting for transfers between devices: 34.2 us -> 0 us
  other arithmetic: 16.3 us -> 0 us
  starting transfers between devices: 15.7 us -> 0 us
  between operations: 14.4 us -> 0.65 us
    psum x1 -> x0, blocking collectives: 130 us -> none  [on_device(): summed = lax.psum(shared, 'tm')]
    pallas_call x0 -> x1, Pallas kernels: none -> 77 us  [on_device(): pl.pallas_call(kernel, out_shape=(tile, tile, tile, shard, shard), in_spe...]
    dot_general x20 -> x0, matrix products: 36.2 us -> none  [the longest x4 10.9 us: block_grads(): jnp.einsum('qhd,khd->hqk', grad_heads, value_heads, preferred_element_typ...]
    all_gather x1 -> x0, waiting for transfers between devices: 34.1 us -> none  [on_device(): lax.all_gather(jnp.stack([text_keys, text_values]), 'space', axis=1, tile...]
    ppermute x4 -> x0, starting transfers between devices: 15.6 us -> none  [the longest x2 8.38 us: from_behind(): lax.ppermute(value, axis, [(source, source + steps) for source in range(l...]
    another operation x7 -> x0, local copies, waits for them, and re-layouts: 15.3 us -> none  [the longest x2 6.06 us: on_device(): text_terms = jnp.stack([textual[1], textual[2]])]
    slice x3 -> x0, local copies, waits for them, and re-layouts: 10.5 us -> none  [the longest x1 5.77 us: on_device(): text_both[1]]
    another operation x5 -> x0, other arithmetic: 10.1 us -> none  [the longest x1 3.74 us: on_device(): text_terms = jnp.stack([textual[1], textual[2]])]
  transfers between devices with their start and end apart: 6 -> 0, of which waited for: 1 -> 0; matrix products, arithmetic and copies ran while one was open for 33% -> 0% of each run, Pallas kernels for 0% -> 0%
where the time goes in v1:
time: 85.4 us; the launch traced here: 85.1 us
  Pallas kernels  77 us (90%)
  local copies, waits for them, and re-layouts  7.42 us (9%)
    pallas_call x1, Pallas kernels, on_device(): pl.pallas_call(kernel, out_shape=(tile, tile, tile, shard, shard), in_spe...  77 us
    unnamed x14, local copies, waits for them, and re-layouts  7.42 us

profile of v1, /device:TPU:1, one launch (start us, length us, event | category | flops | bytes accessed | tf_op | source)
XLA Modules:
  0.0 85.1 jit_solution(6964576850763629120)
XLA Ops:
  0.6 1.3 %copy_bitcast_fusion = (f32[12,256]{1,0:T(8,128)}, f32[12,256]{1,0:T(8,128)}) fusion(f32[1,1,12,256]{3,1,2,0:T(1,128)} %param.14, f32[1,1,12,256]{3,1,2,0:T(1,128)} %param.13), kind=kLoop, calls=%fused_computation | loop fusion | bytes 49152
  2.0 77.0 %shard_map.128 = (bf16[256,1536]{1,0:T(8,128)(2,1)}, bf16[256,1536]{1,0:T(8,128)(2,1)}, bf16[256,1536]{1,0:T(8,128)(2,1)}, bf16[32,1536]{1,0:T(8,128)(2,1)}, bf16[32,1536]{1,0:T(8,128)(2,1)}) custom-call(bf16[256,1536]{1,0:T(8,128)(2,1)} %bitcast.15, bf16[256,1536]{1,0:T(8,128)(2,1)} %bitcast.16, bf16[256,1536]{1,0:T(8,128)(2,1)} %bitcast.17, ...), custom_call_target="tpu_custom_call" | custom-call | tf_op jit(solution)/shard_map/pallas_call | solution.py:408
  79.0 0.0 copy-start.1
  79.0 2.1 %copy.23 = bf16[1,1,256,1536]{3,2,1,0:T(8,128)(2,1)} copy(bf16[1,1,256,1536]{3,2,1,0:T(8,128)(2,1)} %bitcast.14) | data formatting | bytes 1572864
  81.2 0.0 copy-done.1
  81.2 0.0 copy-start
  81.2 0.9 %copy.24 = bf16[1,1,256,1536]{3,2,1,0:T(8,128)(2,1)} copy(bf16[1,1,256,1536]{3,2,1,0:T(8,128)(2,1)S(1)} %bitcast.13) | data formatting | bytes 1572864
  82.0 0.5 copy-done
  82.6 0.0 copy-start.3
  82.6 0.9 %copy.25 = bf16[1,1,256,1536]{3,2,1,0:T(8,128)(2,1)} copy(bf16[1,1,256,1536]{3,2,1,0:T(8,128)(2,1)S(1)} %bitcast.12) | data formatting | bytes 1572864
  83.5 0.1 copy-done.3
  83.5 0.0 copy-start.2
  83.5 0.6 copy.26
  84.2 0.3 copy-done.2
  84.5 0.6 copy.27
Async XLA Ops:
  79.0 2.1 %copy-start.1 = (bf16[256,1536]{1,0:T(8,128)(2,1)S(1)}, bf16[256,1536]{1,0:T(8,128)(2,1)}, u32[]{:S(2)}) copy-start(bf16[256,1536]{1,0:T(8,128)(2,1)} %get-tuple-element.11) | copy-start | bytes 2359300
  81.2 1.4 %copy-start = (bf16[256,1536]{1,0:T(8,128)(2,1)S(1)}, bf16[256,1536]{1,0:T(8,128)(2,1)}, u32[]{:S(2)}) copy-start(bf16[256,1536]{1,0:T(8,128)(2,1)} %get-tuple-element.12) | copy-start | bytes 2359300
  82.6 1.0 %copy-start.3 = (bf16[32,1536]{1,0:T(8,128)(2,1)S(1)}, bf16[32,1536]{1,0:T(8,128)(2,1)}, u32[]{:S(2)}) copy-start(bf16[32,1536]{1,0:T(8,128)(2,1)} %get-tuple-element.25) | copy-start | bytes 294916
  83.5 0.9 %copy-start.2 = (bf16[32,1536]{1,0:T(8,128)(2,1)S(1)}, bf16[32,1536]{1,0:T(8,128)(2,1)}, u32[]{:S(2)}) copy-start(bf16[32,1536]{1,0:T(8,128)(2,1)} %get-tuple-element.26) | copy-start | bytes 294916

commit v2 on v1

v2 whole, which is shorter than its diff:
```python
import functools
import math

import jax
import jax.numpy as jnp
from jax import lax
from jax.experimental import pallas as pl
from jax.experimental.pallas import tpu as pltpu
from jax.sharding import PartitionSpec as P

MESH = pl.DeviceIdType.MESH
BF16 = jnp.bfloat16
F32 = jnp.float32
HEADS = 12
HEAD = 128
ROWS = 256
WIDTH = HEADS * HEAD
TEXT = 256
TOUCH = 128
SHARD = 32
FACTOR = HEAD**-0.5
LOG2E = math.log2(math.e)
GROUP = 4
CHUNK = 2
NEAR = 2
TEXTUAL = 3
TILE = 16
AT_TEXT, AT_PAIR, AT_X = 0, 1, 2


def rnd(value):
    return value.astype(BF16).astype(F32)


def dot_nt(a, b):
    return lax.dot_general(a, b, (((1,), (1,)), ((), ())), preferred_element_type=F32)


def dot_nn(a, b):
    return lax.dot_general(a, b, (((1,), (0,)), ((), ())), preferred_element_type=F32)


def dot_tn(a, b):
    return lax.dot_general(a, b, (((0,), (0,)), ((), ())), preferred_element_type=F32)


def pair(queries, grads, sums_row, delta_row, keys, values):
    scores = dot_nt(keys, queries)
    weights = jnp.exp2(scores * (FACTOR * LOG2E) - sums_row * LOG2E)
    d_values = dot_nn(weights.astype(BF16), grads)
    d_weights = dot_nt(values, grads)
    d_scores = (weights * (d_weights - delta_row)).astype(BF16)
    d_keys = dot_nn(d_scores, queries) * FACTOR
    d_query = (dot_tn(d_scores, keys) * FACTOR).astype(BF16)
    return d_query, d_keys, d_values


def kernel(
    q_hbm, k_hbm, v_hbm, g_hbm, sums_hbm, delta_hbm, tk_hbm, tv_hbm, touch_hbm,
    dq_out, dk_out, dv_out, tk_out, tv_out,
    tiles, sums, delta, k_own, v_own, text, touch,
    dq_acc, dk_acc, dv_acc, dq_sent, dq_back,
    text_f32, text_b16, text_pair, text_sum, x_part, x_sum, tile_part, final, wide, text_done,
    load_sem, qg_send, qg_recv, st_send, st_recv, fast_send, fast_recv, dqf_sem, dqs_send, dqs_recv,
    gather_send, relay_send, gather_recv, fwd_send, fwd_recv, pair_send, pair_recv, x_send, x_recv,
    tile_send, tile_recv, zg_send, zg_recv, done_send, done_recv,
):
    t = lax.axis_index("tm")
    s = lax.axis_index("space")
    core = t % 2
    z = (t // 2) % 8
    y_hi = t // 16
    x = s % 4
    y = y_hi * 2 + s // 4
    me = y * 4 + x
    fast = (t + 1 - 2 * core, s)
    slow_t = t - 1 + 2 * core
    has_slow = jnp.logical_and(slow_t >= 0, slow_t < 32)
    slow = (jnp.where(has_slow, slow_t, t), s)
    far = jnp.logical_or(t == 15, t == 16)
    near = jnp.logical_and(has_slow, jnp.logical_not(far))
    row = s - x
    partner = (s + 4) % 8
    active = y < TEXTUAL
    my_head = jnp.where(active, TEXTUAL * x + y, 0)

    def chip(place, core_at):
        py, px = place // 4, place % 4
        return (((py // 2) * 8 + z) * 2 + core_at, (py % 2) * 4 + px)

    def column(y_at, z_at):
        return (((y_at // 2) * 8 + z_at) * 2 + core, (y_at % 2) * 4 + x)

    def cols(h):
        return pl.ds(pl.multiple_of(h * HEAD, HEAD), HEAD)

    def rows_of(i, size):
        return pl.ds(pl.multiple_of(i * size, size), size)

    def remote(src, dst, send, recv, device):
        return pltpu.make_async_remote_copy(
            src_ref=src, dst_ref=dst, send_sem=send, recv_sem=recv, device_id=device, device_id_type=MESH
        )

    def loop(count, body):
        lax.fori_loop(0, count, lambda i, c: (body(i), c)[1], 0)

    loads = [
        pltpu.make_async_copy(src, dst, load_sem.at[i])
        for i, (src, dst) in enumerate(
            (
                (tk_hbm, text.at[0, rows_of(s, SHARD)]), (tv_hbm, text.at[1, rows_of(s, SHARD)]),
                (q_hbm, tiles.at[0, 0]), (k_hbm, k_own), (g_hbm, tiles.at[0, 1]), (v_hbm, v_own),
                (sums_hbm, sums.at[0]), (delta_hbm, delta.at[0]), (touch_hbm, touch),
            )
        )
    ]
    for load in loads:
        load.start()

    barrier = pltpu.get_barrier_semaphore()

    def greet_plane(i):
        @pl.when(i != me * 2 + core)
        def _():
            pl.semaphore_signal(barrier, 1, device_id=chip(i // 2, i % 2), device_id_type=MESH)

    def greet_column(i):
        @pl.when(i % 8 != z)
        def _():
            pl.semaphore_signal(barrier, 1, device_id=column(i // 8, i % 8), device_id_type=MESH)

    @pl.when(has_slow)
    def _():
        pl.semaphore_signal(barrier, 1, device_id=slow, device_id_type=MESH)

    loop(32, greet_plane)
    loop(32, greet_column)
    pl.semaphore_wait(barrier, 59 + has_slow.astype(jnp.int32))

    def gather(i, owner):
        part = text.at[core, rows_of(owner, SHARD)]
        return remote(part, part, gather_send.at[i], gather_recv.at[owner], (t, i))

    def relay(i, owner):
        part = text.at[core, rows_of(owner, SHARD)]
        return remote(part, part, relay_send.at[i], gather_recv.at[owner], (t, row + i))

    def forward(i):
        part = text.at[core, rows_of(i, SHARD)]
        return remote(part, part, fwd_send.at[i], fwd_recv.at[i], fast)

    def forwarded(i):
        part = text.at[1 - core, rows_of(i, SHARD)]
        return remote(part, part, fwd_send.at[i], fwd_recv.at[i], fast)

    def unless(i, own, body):
        @pl.when(i != own)
        def _():
            body()

    def slow_stats(i):
        src, dst = ((sums_hbm, sums.at[2]), (delta_hbm, delta.at[2]))[i]
        return remote(src, dst, st_send.at[i], st_recv.at[i], slow)

    def slow_tile(i, chunk):
        src = (q_hbm, g_hbm)[i]
        part = pl.ds(pl.multiple_of(chunk * CHUNK * HEAD, CHUNK * HEAD), CHUNK * HEAD)
        return remote(
            src.at[:, part], tiles.at[2, i, :, part], qg_send.at[i, chunk], qg_recv.at[i, chunk], slow
        )

    def fast_copy(i):
        src, dst = (
            (sums_hbm, sums.at[1]), (delta_hbm, delta.at[1]), (q_hbm, tiles.at[1, 0]), (g_hbm, tiles.at[1, 1]),
        )[i]
        return remote(src, dst, fast_send.at[i], fast_recv.at[i], fast)

    for load in loads[:2]:
        load.wait()
    gather(partner, s).start()
    loop(4, lambda i: unless(i, x, lambda: gather(row + i, s).start()))

    def slow_start():
        for i in range(2):
            slow_stats(i).start()

        def send(h):
            slow_tile(0, h).start()
            slow_tile(1, h).start()

        loop(HEADS // CHUNK, send)

    pl.when(near)(slow_start)

    for i in range(4):
        fast_copy(i).start()
    for load in loads[2:]:
        load.wait()

    def heads_of(slot, group, count):
        heads = [group * count + i for i in range(count)]
        return heads, [
            pair(
                tiles[slot, 0, :, cols(h)], tiles[slot, 1, :, cols(h)], sums[slot, h], delta[slot, h],
                k_own[:, cols(h)], v_own[:, cols(h)],
            )
            for h in heads
        ]

    def own_heads(group):
        for h, (dq, dk, dv) in zip(*heads_of(0, group, GROUP)):
            dq_acc[:, cols(h)] = dq.astype(F32)
            dk_acc[:, cols(h)] = rnd(dk)
            dv_acc[:, cols(h)] = rnd(dv)

    loop(HEADS // GROUP, own_heads)
    gather(partner, partner).wait_recv()
    loop(4, lambda i: unless(i, x, lambda: relay(i, partner).start()))
    pl.when(far)(slow_start)

    def near_heads(slot, group, count):
        for h, (dq, dk, dv) in zip(*heads_of(slot, group, count)):
            dq_sent[slot - 1, :, cols(h)] = dq
            dk_acc[:, cols(h)] += rnd(dk)
            dv_acc[:, cols(h)] += rnd(dv)

    for i in range(4):
        fast_copy(i).wait_recv()
    loop(HEADS // GROUP, lambda group: near_heads(1, group, GROUP))
    dq_fast = remote(dq_sent.at[0], dq_back.at[0], dqf_sem.at[0], dqf_sem.at[1], fast)
    dq_fast.start()

    def hand_over(i):
        @pl.when(i != partner)
        def _():
            gather(i, i).wait_recv()

        forward(i).start()

    loop(8, lambda i: unless(i, s, lambda: hand_over(i)))

    def wide_cols(group):
        return pl.ds(pl.multiple_of(group * TEXTUAL * HEAD, TEXTUAL * HEAD), TEXTUAL * HEAD)

    def pair_copy(group):
        return remote(
            text_b16.at[1 - core, :, wide_cols(group)], text_pair.at[:, wide_cols(group)],
            pair_send.at[group], pair_recv.at[group], fast,
        )

    def token_rows():
        token = lax.broadcasted_iota(jnp.int32, (TEXT, TOUCH), 0)
        return jnp.where(token == touch[...], 1.0, 0.0).astype(F32)

    def along_x(i, src):
        return remote(
            text_sum.at[:, wide_cols(i)], x_part.at[src], x_send.at[i], x_recv.at[src], (t, row + i)
        )

    def pair_sum(group):
        pair_copy(group).wait_recv()
        part = wide_cols(group)
        text_sum[:, part] = (text_f32[core, :, part] + text_pair[:, part].astype(F32)).astype(BF16)
        unless(group, x, lambda: along_x(group, x).start())

    def to_owner(i, src):
        return remote(
            x_sum.at[rows_of(i % 8, TILE), cols(i // 8)], tile_part.at[src],
            tile_send.at[i], tile_recv.at[src], column(i // 8, i % 8),
        )

    def x_total():
        loop(4, lambda i: unless(i, x, lambda: along_x(x, i).wait_recv()))
        x_part[x] = text_sum[:, wide_cols(x)]
        total = x_part[0].astype(F32)
        for i in range(1, 4):
            total = total + x_part[i].astype(F32)
        x_sum[...] = total.astype(BF16)
        loop(8 * TEXTUAL, lambda i: unless(i, y * 8 + z, lambda: to_owner(i, y * 8 + z).start()))

    def text_block():
        loop(8, lambda i: unless(i, s, lambda: forwarded(i).wait_recv()))
        pick = token_rows().T.astype(BF16)

        def group_heads(group):
            heads = [group * TEXTUAL + i for i in range(TEXTUAL)]
            keys = [dot_nn(pick, text[0, :, cols(h)]).astype(BF16) for h in heads]
            values = [dot_nn(pick, text[1, :, cols(h)]).astype(BF16) for h in heads]
            terms = [
                pair(tiles[0, 0, :, cols(h)], tiles[0, 1, :, cols(h)], sums[0, h], delta[0, h], keys[i], values[i])
                for i, h in enumerate(heads)
            ]
            for h, (dq, dk, dv) in zip(heads, terms):
                dq_acc[:, cols(h)] += dq.astype(F32)
                text_f32[0, :, cols(h)] = dk
                text_f32[1, :, cols(h)] = dv
                text_b16[0, :, cols(h)] = dk.astype(BF16)
                text_b16[1, :, cols(h)] = dv.astype(BF16)
            pair_copy(group).start()

            @pl.when(group >= 1)
            def _():
                pair_sum(group - 1)

        loop(HEADS // TEXTUAL, group_heads)

    def dq_slow(group):
        part = pl.ds(pl.multiple_of(group * NEAR * HEAD, NEAR * HEAD), NEAR * HEAD)
        return remote(
            dq_sent.at[1, :, part], dq_back.at[1, :, part], dqs_send.at[group], dqs_recv.at[group], slow
        )

    def slow_heads(group):
        pl.when(group == AT_TEXT)(text_block)
        pl.when(group == AT_PAIR)(lambda: pair_sum(HEADS // TEXTUAL - 1))
        pl.when(group == AT_X)(x_total)

        @pl.when(has_slow)
        def _():
            @pl.when(group == 0)
            def _():
                for i in range(2):
                    slow_stats(i).wait_recv()

            @pl.when(group * NEAR % CHUNK == 0)
            def _():
                slow_tile(0, group * NEAR // CHUNK).wait_recv()
                slow_tile(1, group * NEAR // CHUNK).wait_recv()

            near_heads(2, group, NEAR)

            pl.when(near)(lambda: dq_slow(group).start())

        part = pl.ds(pl.multiple_of(group * NEAR * HEAD, NEAR * HEAD), NEAR * HEAD)
        dk_out[:, part] = dk_acc[:, part].astype(BF16)
        dv_out[:, part] = dv_acc[:, part].astype(BF16)

    loop(HEADS // NEAR, slow_heads)

    def z_spread(i, src):
        part = final.at[rows_of(src, TILE)]
        return remote(part, part, zg_send.at[i], zg_recv.at[src], column(y, i))

    def deliver(i, head, core_at):
        place = i // 2
        owner = (place // 4 % 2) * 4 + place % 4
        return remote(
            wide.at[rows_of(owner, SHARD)], text_done.at[core_at, :, cols(head)],
            done_send.at[i], done_recv.at[core_at * HEADS + head], chip(place, i % 2),
        )

    @pl.when(active)
    def _():
        at = y * 8 + z
        tile_part[at] = x_sum[rows_of(z, TILE), cols(y)]
        loop(32, lambda i: unless(i, at, lambda: to_owner(at, i).wait_recv()))
        total = tile_part[0].astype(F32)
        for i in range(1, 32):
            total = total + tile_part[i].astype(F32)
        final[rows_of(z, TILE), :] = total.astype(BF16)
        loop(8, lambda i: unless(i, z, lambda: z_spread(i, z).start()))

    pl.when(far)(lambda: loop(HEADS // NEAR, lambda group: dq_slow(group).start()))

    @pl.when(active)
    def _():
        loop(8, lambda i: unless(i, z, lambda: z_spread(z, i).wait_recv()))
        wide[...] = dot_nn(token_rows().astype(BF16), final[...]).astype(BF16)
        loop(32, lambda i: unless(i, me * 2 + core, lambda: deliver(i, my_head, core).start()))
        text_done[core, :, cols(my_head)] = wide[rows_of(s, SHARD), :]

    dq_fast.wait_recv()

    def finish(group):
        part = pl.ds(pl.multiple_of(group * NEAR * HEAD, NEAR * HEAD), NEAR * HEAD)
        both = dq_acc[:, part] + dq_back[0, :, part].astype(F32)

        @pl.when(has_slow)
        def _():
            dq_slow(group).wait_recv()
            dq_out[:, part] = (both + dq_back[1, :, part].astype(F32)).astype(BF16)

        @pl.when(jnp.logical_not(has_slow))
        def _():
            dq_out[:, part] = both.astype(BF16)

    loop(HEADS // NEAR, finish)

    for i in range(4):
        fast_copy(i).wait_send()
    dq_fast.wait_send()
    loop(HEADS // TEXTUAL, lambda group: pair_copy(group).wait_send())
    gather(partner, s).wait_send()
    loop(8, lambda i: unless(i, s, lambda: forward(i).wait_send()))

    def x_sent(i):
        gather(row + i, s).wait_send()
        relay(i, partner).wait_send()
        along_x(i, x).wait_send()

    loop(4, lambda i: unless(i, x, lambda: x_sent(i)))
    loop(8 * TEXTUAL, lambda i: unless(i, y * 8 + z, lambda: to_owner(i, y * 8 + z).wait_send()))

    @pl.when(has_slow)
    def _():
        for i in range(2):
            slow_stats(i).wait_send()

        def sent(h):
            slow_tile(0, h).wait_send()
            slow_tile(1, h).wait_send()

        loop(HEADS // CHUNK, sent)
        loop(HEADS // NEAR, lambda group: dq_slow(group).wait_send())

    @pl.when(active)
    def _():
        loop(8, lambda i: unless(i, z, lambda: z_spread(i, z).wait_send()))
        loop(32, lambda i: unless(i, me * 2 + core, lambda: deliver(i, my_head, core).wait_send()))

    def done_from(i):
        head, core_at = i % HEADS, i // HEADS
        own = jnp.logical_and(jnp.logical_and(active, head == my_head), core_at == core)

        @pl.when(jnp.logical_not(own))
        def _():
            deliver(me * 2 + core, head, core_at).wait_recv()

    loop(2 * HEADS, done_from)
    tk_out[...] = text_done[0]
    tv_out[...] = text_done[1]


def store(*refs):
    count = (len(refs) - 1) // 2
    copies = [
        pltpu.make_async_copy(refs[i], refs[count + i], refs[-1].at[i]) for i in range(count)
    ]
    for copy in copies:
        copy.start()
    for copy in copies:
        copy.wait()


def on_device(query_tiles, key_tiles, value_tiles, grad_tiles, log_sums, row_delta, text_keys, text_values, touch_list):
    shapes = [(ROWS, WIDTH)] * 3 + [(SHARD, WIDTH)] * 2
    dma = pltpu.SemaphoreType.DMA
    held = pl.pallas_call(
        kernel,
        out_shape=[pltpu.VMEM(shape, BF16) for shape in shapes],
        in_specs=[pl.BlockSpec(memory_space=pl.ANY)] * 9,
        out_specs=[pl.BlockSpec(memory_space=pltpu.VMEM)] * 5,
        scratch_shapes=[
            pltpu.VMEM((3, 2, ROWS, WIDTH), BF16),
            pltpu.VMEM((3, HEADS, 1, ROWS), F32),
            pltpu.VMEM((3, HEADS, 1, ROWS), F32),
            pltpu.VMEM((ROWS, WIDTH), BF16),
            pltpu.VMEM((ROWS, WIDTH), BF16),
            pltpu.VMEM((2, TEXT, WIDTH), BF16),
            pltpu.VMEM((1, TOUCH), jnp.int32),
            pltpu.VMEM((ROWS, WIDTH), F32),
            pltpu.VMEM((ROWS, WIDTH), F32),
            pltpu.VMEM((ROWS, WIDTH), F32),
            pltpu.VMEM((2, ROWS, WIDTH), BF16),
            pltpu.VMEM((2, ROWS, WIDTH), BF16),
            pltpu.VMEM((2, TOUCH, WIDTH), F32),
            pltpu.VMEM((2, TOUCH, WIDTH), BF16),
            pltpu.VMEM((TOUCH, WIDTH), BF16),
            pltpu.VMEM((TOUCH, WIDTH), BF16),
            pltpu.VMEM((4, TOUCH, TEXTUAL * HEAD), BF16),
            pltpu.VMEM((TOUCH, TEXTUAL * HEAD), BF16),
            pltpu.VMEM((32, TILE, HEAD), BF16),
            pltpu.VMEM((TOUCH, HEAD), BF16),
            pltpu.VMEM((TEXT, HEAD), BF16),
            pltpu.VMEM((2, SHARD, WIDTH), BF16),
            dma((9,)),
            dma((2, HEADS)), dma((2, HEADS)),
            dma((2,)), dma((2,)),
            dma((4,)), dma((4,)),
            dma((2,)),
            dma((HEADS // NEAR,)), dma((HEADS // NEAR,)),
            dma((8,)), dma((4,)), dma((8,)),
            dma((8,)), dma((8,)),
            dma((HEADS // TEXTUAL,)), dma((HEADS // TEXTUAL,)),
            dma((4,)), dma((4,)),
            dma((8 * TEXTUAL,)), dma((32,)),
            dma((8,)), dma((8,)),
            dma((32,)), dma((2 * HEADS,)),
        ],
        compiler_params=pltpu.CompilerParams(
            collective_id=0, has_side_effects=True, vmem_limit_bytes=48 << 20
        ),
    )(
        *(
            pltpu.with_memory_space_constraint(value, pltpu.HBM)
            for value in (
                query_tiles[0, 0], key_tiles[0, 0], value_tiles[0, 0], grad_tiles[0, 0],
                log_sums.reshape(HEADS, 1, ROWS), row_delta.reshape(HEADS, 1, ROWS),
                text_keys, text_values, touch_list[0],
            )
        )
    )
    dq, dk, dv, tk, tv = pl.pallas_call(
        store,
        out_shape=[jax.ShapeDtypeStruct(shape, BF16) for shape in shapes],
        in_specs=[pl.BlockSpec(memory_space=pltpu.VMEM)] * 5,
        out_specs=[pl.BlockSpec(memory_space=pl.ANY)] * 5,
        scratch_shapes=[pltpu.SemaphoreType.DMA((5,))],
    )(*(pltpu.with_memory_space_constraint(value, pltpu.VMEM) for value in held))
    return dq[None, None], dk[None, None], dv[None, None], tk, tv


def solution(mesh):
    tile = P("tm", "space", None, None)
    return jax.shard_map(
        on_device,
        mesh=mesh,
        in_specs=(tile,) * 6 + (P("space", None), P("space", None), P("tm", "space", None)),
        out_specs=(tile, tile, tile, P("space", None), P("space", None)),
        check_vma=False,
    )
```

time: 85.4 us -> 61.2 us (0.72)
  the two profiles are of different devices: /device:TPU:1 before, /device:TPU:30 now
where the time goes in v2:
time: 61.2 us; the launch traced here: 61.1 us
  Pallas kernels  60.5 us (99%)
  between operations  0.64 us (1%)
    pallas_call x1, Pallas kernels, on_device(): pl.pallas_call(kernel, out_shape=[pltpu.VMEM(shape, BF16) for shape in sh...  59 us
    pallas_call x1, Pallas kernels, on_device(): pl.pallas_call(store, out_shape=[jax.ShapeDtypeStruct(shape, BF16) for sh...  1.5 us

profile of v2, /device:TPU:30, one launch (start us, length us, event | category | flops | bytes accessed | tf_op | source)
XLA Modules:
  0.0 61.1 jit_solution(2608795246371422287)
XLA Ops:
  0.6 59.0 %shard_map.128 = (bf16[256,1536]{1,0:T(8,128)(2,1)S(1)}, bf16[256,1536]{1,0:T(8,128)(2,1)S(1)}, bf16[256,1536]{1,0:T(8,128)(2,1)S(1)}, bf16[32,1536]{1,0:T(8,128)(2,1)S(1)}, bf16[32,1536]{1,0:T(8,128)(2,1)S(1)}) custom-call(bf16[256,1536]{1,0:T(8,128)(2,1)} %bitcast.10, bf16[256,1536]{1,0:T(8,128)(2,1)} %bitcast.11, bf16[256,1536]{1,0:T(8,128)(2,1)} %bitcast.12, ...), custom_call_target="tpu_custom_call" | custom-call | tf_op jit(solution)/shard_map/pallas_call | solution.py:449
  59.6 1.5 %shard_map.129 = (bf16[256,1536]{1,0:T(8,128)(2,1)}, bf16[256,1536]{1,0:T(8,128)(2,1)}, bf16[256,1536]{1,0:T(8,128)(2,1)}, bf16[32,1536]{1,0:T(8,128)(2,1)}, bf16[32,1536]{1,0:T(8,128)(2,1)}) custom-call(bf16[256,1536]{1,0:T(8,128)(2,1)S(1)} %get-tuple-element.15.refs_0_, bf16[256,1536]{1,0:T(8,128)(2,1)S(1)} %get-tuple-element.16.refs_1_, ...), custom_call_target="tpu_custom_call" | custom-call | tf_op jit(solution)/shard_map/pallas_call | solution.py:504

commit v3 on v2

--- a/solution.py
+++ b/solution.py
@@ -25,7 +25,7 @@
 NEAR = 2
 TEXTUAL = 3
 TILE = 16
-AT_TEXT, AT_PAIR, AT_X = 0, 1, 2
+AT_TEXT, AT_X, AT_TILE = 0, 1, 4
 
 
 def rnd(value):
@@ -61,8 +61,8 @@
     tiles, sums, delta, k_own, v_own, text, touch,
     dq_acc, dk_acc, dv_acc, dq_sent, dq_back,
     text_f32, text_b16, text_pair, text_sum, x_part, x_sum, tile_part, final, wide, text_done,
-    load_sem, qg_send, qg_recv, st_send, st_recv, fast_send, fast_recv, dqf_sem, dqs_send, dqs_recv,
-    gather_send, relay_send, gather_recv, fwd_send, fwd_recv, pair_send, pair_recv, x_send, x_recv,
+    known, load_sem, text_sem, qg_send, qg_recv, st_send, st_recv, fast_send, fast_recv, dqf_sem, dqs_send, dqs_recv,
+    gather_send, gather_recv, fwd_send, fwd_recv, pair_send, pair_recv, x_send, x_recv,
     tile_send, tile_recv, zg_send, zg_recv, done_send, done_recv,
 ):
     t = lax.axis_index("tm")
@@ -92,9 +92,13 @@
         return (((y_at // 2) * 8 + z_at) * 2 + core, (y_at % 2) * 4 + x)
 
     def cols(h):
+        if isinstance(h, int):
+            return pl.ds(h * HEAD, HEAD)
         return pl.ds(pl.multiple_of(h * HEAD, HEAD), HEAD)
 
     def rows_of(i, size):
+        if isinstance(i, int):
+            return pl.ds(i * size, size)
         return pl.ds(pl.multiple_of(i * size, size), size)
 
     def remote(src, dst, send, recv, device):
@@ -104,55 +108,85 @@
 
     def loop(count, body):
         lax.fori_loop(0, count, lambda i, c: (body(i), c)[1], 0)
+
+    def each(count, body):
+        for i in range(count):
+            body(i)
+
+    barrier = pltpu.get_barrier_semaphore()
+    along_row_at = [(t, row + (x + i) % 4) for i in range(1, 4)]
+    beside_y = [column((y + i) % 4, z) for i in (1, 3)]
+    beside_z = [column(y, (z + i) % 8) for i in (1, 7)]
+    for device in along_row_at + beside_y + beside_z + [fast]:
+        pl.semaphore_signal(barrier, 1, device_id=device, device_id_type=MESH)
+
+    @pl.when(has_slow)
+    def _():
+        pl.semaphore_signal(barrier, 1, device_id=slow, device_id_type=MESH)
+
+    rounds = [beside_z] * 3 + [beside_y] * 2 + [[fast], along_row_at]
+
+    def spread_word(i):
+        if i > 0:
+            pl.semaphore_wait(known.at[i - 1], len(rounds[i - 1]))
+        if i < len(rounds):
+            for device in rounds[i]:
+                pl.semaphore_signal(known.at[i], 1, device_id=device, device_id_type=MESH)
 
     loads = [
         pltpu.make_async_copy(src, dst, load_sem.at[i])
         for i, (src, dst) in enumerate(
             (
-                (tk_hbm, text.at[0, rows_of(s, SHARD)]), (tv_hbm, text.at[1, rows_of(s, SHARD)]),
                 (q_hbm, tiles.at[0, 0]), (k_hbm, k_own), (g_hbm, tiles.at[0, 1]), (v_hbm, v_own),
                 (sums_hbm, sums.at[0]), (delta_hbm, delta.at[0]), (touch_hbm, touch),
             )
         )
     ]
+    own_text = text.at[core, rows_of(s, SHARD)]
+
+    @pl.when(core == 0)
+    def _():
+        pltpu.make_async_copy(tk_hbm, own_text, text_sem).start()
+
+    @pl.when(core == 1)
+    def _():
+        pltpu.make_async_copy(tv_hbm, own_text, text_sem).start()
+
     for load in loads:
         load.start()
 
-    barrier = pltpu.get_barrier_semaphore()
-
-    def greet_plane(i):
-        @pl.when(i != me * 2 + core)
-        def _():
-            pl.semaphore_signal(barrier, 1, device_id=chip(i // 2, i % 2), device_id_type=MESH)
-
-    def greet_column(i):
-        @pl.when(i % 8 != z)
-        def _():
-            pl.semaphore_signal(barrier, 1, device_id=column(i // 8, i % 8), device_id_type=MESH)
-
-    @pl.when(has_slow)
-    def _():
-        pl.semaphore_signal(barrier, 1, device_id=slow, device_id_type=MESH)
-
-    loop(32, greet_plane)
-    loop(32, greet_column)
-    pl.semaphore_wait(barrier, 59 + has_slow.astype(jnp.int32))
-
-    def gather(i, owner):
-        part = text.at[core, rows_of(owner, SHARD)]
-        return remote(part, part, gather_send.at[i], gather_recv.at[owner], (t, i))
-
-    def relay(i, owner):
-        part = text.at[core, rows_of(owner, SHARD)]
-        return remote(part, part, relay_send.at[i], gather_recv.at[owner], (t, row + i))
-
-    def forward(i):
-        part = text.at[core, rows_of(i, SHARD)]
-        return remote(part, part, fwd_send.at[i], fwd_recv.at[i], fast)
-
-    def forwarded(i):
-        part = text.at[1 - core, rows_of(i, SHARD)]
-        return remote(part, part, fwd_send.at[i], fwd_recv.at[i], fast)
+    pl.semaphore_wait(barrier, 8 + has_slow.astype(jnp.int32))
+    spread_word(0)
+
+    def half(i):
+        return pl.ds(i * WIDTH // 2, WIDTH // 2)
+
+    def gather(i, owner, at, sem):
+        part = text.at[core, rows_of(owner, SHARD), half(at)]
+        return remote(part, part, gather_send.at[sem, at], gather_recv.at[owner, at], (t, i))
+
+    def along_row(i, owner, at):
+        return gather(row + i, owner, at, i)
+
+    def relay(i, at):
+        return gather(row + i, partner, at, 5 + i)
+
+    def to_partner(owner, at):
+        return gather(partner, owner, at, 4)
+
+    def forward(array, first, block, at):
+        part = text.at[array, pl.ds(pl.multiple_of(first, 4 * SHARD), 4 * SHARD), half(at)]
+        return remote(part, part, fwd_send.at[block, at], fwd_recv.at[block, at], fast)
+
+    def hand_over(at):
+        each(4, lambda i: unless(i, x, lambda: along_row(i, row + i, at).wait_recv()))
+        forward(core, row * SHARD, 0, at).start()
+        each(4, lambda i: unless(i, x, lambda: along_row(i, 4 - row + i, at).wait_recv()))
+        forward(core, (4 - row) * SHARD, 1, at).start()
+
+    def handed(at):
+        for block, first in enumerate((row, 4 - row)):
+            forward(1 - core, first * SHARD, block, at).wait_recv()
 
     def unless(i, own, body):
         @pl.when(i != own)
@@ -176,10 +210,10 @@
         )[i]
         return remote(src, dst, fast_send.at[i], fast_recv.at[i], fast)
 
-    for load in loads[:2]:
-        load.wait()
-    gather(partner, s).start()
-    loop(4, lambda i: unless(i, x, lambda: gather(row + i, s).start()))
+    pltpu.make_async_copy(tk_hbm, own_text, text_sem).wait()
+    for at in range(2):
+        to_partner(s, at).start()
+        each(4, lambda i: unless(i, x, lambda: along_row(i, s, at).start()))
 
     def slow_start():
         for i in range(2):
@@ -195,7 +229,7 @@
 
     for i in range(4):
         fast_copy(i).start()
-    for load in loads[2:]:
+    for load in loads:
         load.wait()
 
     def heads_of(slot, group, count):
@@ -208,16 +242,26 @@
             for h in heads
         ]
 
+    def relay_partner():
+        for at in range(2):
+            to_partner(partner, at).wait_recv()
+            each(4, lambda i: unless(i, x, lambda: relay(i, at).start()))
+        pl.when(far)(slow_start)
+
     def own_heads(group):
+        pl.when(group == 1)(lambda: spread_word(1))
+
+        @pl.when(group == 2)
+        def _():
+            spread_word(2)
+            relay_partner()
+
         for h, (dq, dk, dv) in zip(*heads_of(0, group, GROUP)):
             dq_acc[:, cols(h)] = dq.astype(F32)
             dk_acc[:, cols(h)] = rnd(dk)
             dv_acc[:, cols(h)] = rnd(dv)
 
     loop(HEADS // GROUP, own_heads)
-    gather(partner, partner).wait_recv()
-    loop(4, lambda i: unless(i, x, lambda: relay(i, partner).start()))
-    pl.when(far)(slow_start)
 
     def near_heads(slot, group, count):
         for h, (dq, dk, dv) in zip(*heads_of(slot, group, count)):
@@ -227,18 +271,18 @@
 
     for i in range(4):
         fast_copy(i).wait_recv()
-    loop(HEADS // GROUP, lambda group: near_heads(1, group, GROUP))
+
+    def fast_heads(group):
+        for i in range(HEADS // GROUP):
+            pl.when(group == i)(lambda i=i: spread_word(3 + i))
+        near_heads(1, group, GROUP)
+
+    loop(HEADS // GROUP, fast_heads)
+    spread_word(6)
     dq_fast = remote(dq_sent.at[0], dq_back.at[0], dqf_sem.at[0], dqf_sem.at[1], fast)
     dq_fast.start()
 
-    def hand_over(i):
-        @pl.when(i != partner)
-        def _():
-            gather(i, i).wait_recv()
-
-        forward(i).start()
-
-    loop(8, lambda i: unless(i, s, lambda: hand_over(i)))
+    hand_over(0)
 
     def wide_cols(group):
         return pl.ds(pl.multiple_of(group * TEXTUAL * HEAD, TEXTUAL * HEAD), TEXTUAL * HEAD)
@@ -262,7 +306,9 @@
         pair_copy(group).wait_recv()
         part = wide_cols(group)
         text_sum[:, part] = (text_f32[core, :, part] + text_pair[:, part].astype(F32)).astype(BF16)
-        unless(group, x, lambda: along_x(group, x).start())
+
+    def group_at(step):
+        return (x + 1 + step) % 4
 
     def to_owner(i, src):
         return remote(
@@ -271,19 +317,23 @@
         )
 
     def x_total():
-        loop(4, lambda i: unless(i, x, lambda: along_x(x, i).wait_recv()))
+        pair_sum(x)
+        each(4, lambda i: unless(i, x, lambda: along_x(x, i).wait_recv()))
         x_part[x] = text_sum[:, wide_cols(x)]
         total = x_part[0].astype(F32)
         for i in range(1, 4):
             total = total + x_part[i].astype(F32)
         x_sum[...] = total.astype(BF16)
-        loop(8 * TEXTUAL, lambda i: unless(i, y * 8 + z, lambda: to_owner(i, y * 8 + z).start()))
+        each(8 * TEXTUAL, lambda i: unless(i, y * 8 + z, lambda: to_owner(i, y * 8 + z).start()))
 
     def text_block():
-        loop(8, lambda i: unless(i, s, lambda: forwarded(i).wait_recv()))
         pick = token_rows().T.astype(BF16)
-
-        def group_heads(group):
+        hand_over(1)
+        handed(0)
+        handed(1)
+
+        def group_heads(step):
+            group = group_at(step)
             heads = [group * TEXTUAL + i for i in range(TEXTUAL)]
             keys = [dot_nn(pick, text[0, :, cols(h)]).astype(BF16) for h in heads]
             values = [dot_nn(pick, text[1, :, cols(h)]).astype(BF16) for h in heads]
@@ -299,11 +349,27 @@
                 text_b16[1, :, cols(h)] = dv.astype(BF16)
             pair_copy(group).start()
 
-            @pl.when(group >= 1)
+            @pl.when(step >= 1)
             def _():
-                pair_sum(group - 1)
+                before = group_at(step - 1)
+                pair_sum(before)
+                along_x(before, x).start()
 
         loop(HEADS // TEXTUAL, group_heads)
+
+    def z_spread(i, src):
+        part = final.at[rows_of(src, TILE)]
+        return remote(part, part, zg_send.at[i], zg_recv.at[src], column(y, i))
+
+    def tile_total():
+        at = y * 8 + z
+        tile_part[at] = x_sum[rows_of(z, TILE), cols(y)]
+        each(32, lambda i: unless(i, at, lambda: to_owner(at, i).wait_recv()))
+        total = tile_part[0].astype(F32)
+        for i in range(1, 32):
+            total = total + tile_part[i].astype(F32)
+        final[rows_of(z, TILE), :] = total.astype(BF16)
+        each(8, lambda i: unless(i, z, lambda: z_spread(i, z).start()))
 
     def dq_slow(group):
         part = pl.ds(pl.multiple_of(group * NEAR * HEAD, NEAR * HEAD), NEAR * HEAD)
@@ -313,8 +379,11 @@
 
     def slow_heads(group):
         pl.when(group == AT_TEXT)(text_block)
-        pl.when(group == AT_PAIR)(lambda: pair_sum(HEADS // TEXTUAL - 1))
         pl.when(group == AT_X)(x_total)
+        pl.when(jnp.logical_and(active, group == AT_TILE))(tile_total)
+        pl.when(jnp.logical_and(far, group == AT_TILE))(
+            lambda: loop(AT_TILE, lambda before: dq_slow(before).start())
+        )
 
         @pl.when(has_slow)
         def _():
@@ -330,17 +399,13 @@
 
             near_heads(2, group, NEAR)
 
-            pl.when(near)(lambda: dq_slow(group).start())
+            pl.when(jnp.logical_or(near, group >= AT_TILE))(lambda: dq_slow(group).start())
 
         part = pl.ds(pl.multiple_of(group * NEAR * HEAD, NEAR * HEAD), NEAR * HEAD)
         dk_out[:, part] = dk_acc[:, part].astype(BF16)
         dv_out[:, part] = dv_acc[:, part].astype(BF16)
 
     loop(HEADS // NEAR, slow_heads)
-
-    def z_spread(i, src):
-        part = final.at[rows_of(src, TILE)]
-        return remote(part, part, zg_send.at[i], zg_recv.at[src], column(y, i))
 
     def deliver(i, head, core_at):
         place = i // 2
@@ -352,23 +417,15 @@
 
     @pl.when(active)
     def _():
-        at = y * 8 + z
-        tile_part[at] = x_sum[rows_of(z, TILE), cols(y)]
-        loop(32, lambda i: unless(i, at, lambda: to_owner(at, i).wait_recv()))
-        total = tile_part[0].astype(F32)
-        for i in range(1, 32):
-            total = total + tile_part[i].astype(F32)
-        final[rows_of(z, TILE), :] = total.astype(BF16)
-        loop(8, lambda i: unless(i, z, lambda: z_spread(i, z).start()))
-
-    pl.when(far)(lambda: loop(HEADS // NEAR, lambda group: dq_slow(group).start()))
-
-    @pl.when(active)
-    def _():
-        loop(8, lambda i: unless(i, z, lambda: z_spread(z, i).wait_recv()))
+        each(8, lambda i: unless(i, z, lambda: z_spread(z, i).wait_recv()))
+        spread_word(7)
         wide[...] = dot_nn(token_rows().astype(BF16), final[...]).astype(BF16)
-        loop(32, lambda i: unless(i, me * 2 + core, lambda: deliver(i, my_head, core).start()))
+        each(32, lambda i: unless(i, me * 2 + core, lambda: deliver(i, my_head, core).start()))
         text_done[core, :, cols(my_head)] = wide[rows_of(s, SHARD), :]
+
+    @pl.when(jnp.logical_not(active))
+    def _():
+        spread_word(7)
 
     dq_fast.wait_recv()
 
@@ -391,12 +448,15 @@
         fast_copy(i).wait_send()
     dq_fast.wait_send()
     loop(HEADS // TEXTUAL, lambda group: pair_copy(group).wait_send())
-    gather(partner, s).wait_send()
-    loop(8, lambda i: unless(i, s, lambda: forward(i).wait_send()))
+    for at in range(2):
+        to_partner(s, at).wait_send()
+        for block, first in enumerate((row, 4 - row)):
+            forward(core, first * SHARD, block, at).wait_send()
 
     def x_sent(i):
-        gather(row + i, s).wait_send()
-        relay(i, partner).wait_send()
+        for at in range(2):
+            along_row(i, s, at).wait_send()
+            relay(i, at).wait_send()
         along_x(i, x).wait_send()
 
     loop(4, lambda i: unless(i, x, lambda: x_sent(i)))
@@ -427,7 +487,7 @@
         def _():
             deliver(me * 2 + core, head, core_at).wait_recv()
 
-    loop(2 * HEADS, done_from)
+    each(2 * HEADS, done_from)
     tk_out[...] = text_done[0]
     tv_out[...] = text_done[1]
 
@@ -474,14 +534,15 @@
             pltpu.VMEM((TOUCH, HEAD), BF16),
             pltpu.VMEM((TEXT, HEAD), BF16),
             pltpu.VMEM((2, SHARD, WIDTH), BF16),
-            dma((9,)),
+            pltpu.SemaphoreType.REGULAR((7,)),
+            dma((7,)), dma,
             dma((2, HEADS)), dma((2, HEADS)),
             dma((2,)), dma((2,)),
             dma((4,)), dma((4,)),
             dma((2,)),
             dma((HEADS // NEAR,)), dma((HEADS // NEAR,)),
-            dma((8,)), dma((4,)), dma((8,)),
-            dma((8,)), dma((8,)),
+            dma((9, 2)), dma((8, 2)),
+            dma((2, 2)), dma((2, 2)),
             dma((HEADS // TEXTUAL,)), dma((HEADS // TEXTUAL,)),
             dma((4,)), dma((4,)),
             dma((8 * TEXTUAL,)), dma((32,)),

time: 61.2 us -> 56 us (0.915)
  the two profiles are of different devices: /device:TPU:30 before, /device:TPU:1 now
where the time goes in v3:
time: 56 us; the launch traced here: 55.9 us
  Pallas kernels  55.2 us (99%)
  between operations  0.64 us (1%)
    pallas_call x1, Pallas kernels, on_device(): pl.pallas_call(kernel, out_shape=[pltpu.VMEM(shape, BF16) for shape in sh...  53.7 us
    pallas_call x1, Pallas kernels, on_device(): pl.pallas_call(store, out_shape=[jax.ShapeDtypeStruct(shape, BF16) for sh...  1.5 us

profile of v3, /device:TPU:1, one launch (start us, length us, event | category | flops | bytes accessed | tf_op | source)
XLA Modules:
  0.0 55.9 jit_solution(7428631472678114784)
XLA Ops:
  0.6 53.7 %shard_map.128 = (bf16[256,1536]{1,0:T(8,128)(2,1)S(1)}, bf16[256,1536]{1,0:T(8,128)(2,1)S(1)}, bf16[256,1536]{1,0:T(8,128)(2,1)S(1)}, bf16[32,1536]{1,0:T(8,128)(2,1)S(1)}, bf16[32,1536]{1,0:T(8,128)(2,1)S(1)}) custom-call(bf16[256,1536]{1,0:T(8,128)(2,1)} %bitcast.10, bf16[256,1536]{1,0:T(8,128)(2,1)} %bitcast.11, bf16[256,1536]{1,0:T(8,128)(2,1)} %bitcast.12, ...), custom_call_target="tpu_custom_call" | custom-call | tf_op jit(solution)/shard_map/pallas_call | solution.py:509
  54.4 1.5 %shard_map.129 = (bf16[256,1536]{1,0:T(8,128)(2,1)}, bf16[256,1536]{1,0:T(8,128)(2,1)}, bf16[256,1536]{1,0:T(8,128)(2,1)}, bf16[32,1536]{1,0:T(8,128)(2,1)}, bf16[32,1536]{1,0:T(8,128)(2,1)}) custom-call(bf16[256,1536]{1,0:T(8,128)(2,1)S(1)} %get-tuple-element.15.refs_0_, bf16[256,1536]{1,0:T(8,128)(2,1)S(1)} %get-tuple-element.16.refs_1_, ...), custom_call_target="tpu_custom_call" | custom-call | tf_op jit(solution)/shard_map/pallas_call | solution.py:565

commit v4 on v3

--- a/solution.py
+++ b/solution.py
@@ -25,7 +25,7 @@
 NEAR = 2
 TEXTUAL = 3
 TILE = 16
-AT_TEXT, AT_X, AT_TILE = 0, 1, 4
+AT_TEXT, AT_X, AT_TILE = 0, 1, 3
 
 
 def rnd(value):

time: 56 us -> 56.1 us (level)
  no operation moved by 1% of the time
where the time goes in v4:
time: 56.1 us; the launch traced here: 56 us
  Pallas kernels  55.4 us (99%)
  between operations  0.64 us (1%)
    pallas_call x1, Pallas kernels, on_device(): pl.pallas_call(kernel, out_shape=[pltpu.VMEM(shape, BF16) for shape in sh...  53.9 us
    pallas_call x1, Pallas kernels, on_device(): pl.pallas_call(store, out_shape=[jax.ShapeDtypeStruct(shape, BF16) for sh...  1.5 us

profile of v4, /device:TPU:1, one launch (start us, length us, event | category | flops | bytes accessed | tf_op | source)
XLA Modules:
  0.0 56.0 jit_solution(17074494180362306911)
XLA Ops:
  0.6 53.9 %shard_map.128 = (bf16[256,1536]{1,0:T(8,128)(2,1)S(1)}, bf16[256,1536]{1,0:T(8,128)(2,1)S(1)}, bf16[256,1536]{1,0:T(8,128)(2,1)S(1)}, bf16[32,1536]{1,0:T(8,128)(2,1)S(1)}, bf16[32,1536]{1,0:T(8,128)(2,1)S(1)}) custom-call(bf16[256,1536]{1,0:T(8,128)(2,1)} %bitcast.10, bf16[256,1536]{1,0:T(8,128)(2,1)} %bitcast.11, bf16[256,1536]{1,0:T(8,128)(2,1)} %bitcast.12, ...), custom_call_target="tpu_custom_call" | custom-call | tf_op jit(solution)/shard_map/pallas_call | solution.py:509
  54.5 1.5 %shard_map.129 = (bf16[256,1536]{1,0:T(8,128)(2,1)}, bf16[256,1536]{1,0:T(8,128)(2,1)}, bf16[256,1536]{1,0:T(8,128)(2,1)}, bf16[32,1536]{1,0:T(8,128)(2,1)}, bf16[32,1536]{1,0:T(8,128)(2,1)}) custom-call(bf16[256,1536]{1,0:T(8,128)(2,1)S(1)} %get-tuple-element.15.refs_0_, bf16[256,1536]{1,0:T(8,128)(2,1)S(1)} %get-tuple-element.16.refs_1_, ...), custom_call_target="tpu_custom_call" | custom-call | tf_op jit(solution)/shard_map/pallas_call | solution.py:565
